TPU v7x, 32 devices: a whole 2x2x4 slice. The times are simulated.
32 devices in a mesh: dp: 8 (over y, x, core), slab: 4 (over z).
Axes of the slice: x: 2, y: 2, z: 4, core: 2. Of those that a mesh axis runs over, the one named last changes fastest.
Arguments:
- images: bfloat16 [8, 256, 32, 128], P('dp', 'slab'), may hold values from -6 to 6
- cotangent: bfloat16 [8, 128, 64, 256], P('dp', None, 'slab'), may hold values from -6 to 6
- kernel: bfloat16 [3, 3, 256, 128], replicated, may hold values from -0.125 to 0.125
Outputs:
- grad_images: bfloat16 [8, 256, 32, 128], P('dp', 'slab')
- grad_kernel: float32 [3, 3, 256, 128], replicated
All inputs are finite; a program needn't handle non-finite values.
Results may differ from a plain program's by a relative error of at most 0.0034.
Values may be sent and summed in bfloat16 or wider, within the bound.
A program may use at most 64 MiB of HBM per device.

v0:
```python
import jax
import jax.numpy as jnp
from jax import lax
from jax.sharding import PartitionSpec as P


def extended(cells, sides, width):
    for axis, dim in sides:
        count = lax.axis_size(axis)
        ends = count - 1
        head = lax.slice_in_dim(cells, 0, width, axis=dim)
        tail = lax.slice_in_dim(cells, cells.shape[dim] - width, cells.shape[dim], axis=dim)
        cells = jnp.concatenate(
            [
                lax.ppermute(tail, axis, [(i, (i + 1) % count) for i in range(ends)]),
                cells,
                lax.ppermute(head, axis, [((i + 1) % count, i) for i in range(ends)]),
            ],
            axis=dim,
        )
    return cells


def upsample(field):
    return jnp.repeat(jnp.repeat(field, 2, axis=2), 2, axis=3)


def downsum(field):
    count, chans, rows, cols = field.shape
    return field.reshape(count, chans, rows // 2, 2, cols // 2, 2).sum(axis=(3, 5))


def kernel_terms(padded_up, grad_rows):
    return lax.conv_general_dilated(
        padded_up,
        grad_rows,
        (1, 1),
        ((0, 0), (1, 1)),
        dimension_numbers=("CNHW", "IOHW", "HWNC"),
        preferred_element_type=jnp.float32,
    )


def input_terms(padded_grad, kernel):
    flipped = kernel[::-1, ::-1]
    return lax.conv_general_dilated(
        padded_grad,
        flipped,
        (1, 1),
        ((0, 0), (1, 1)),
        dimension_numbers=("NCHW", "HWOI", "NCHW"),
        preferred_element_type=jnp.float32,
    )


def body(images, cotangent, kernel):
    slab_low = lax.all_to_all(images, "slab", split_axis=2, concat_axis=1, tiled=True)
    slab_up = upsample(slab_low)
    padded_up = extended(slab_up, (("slab", 2),), 1)
    padded_grad = extended(cotangent, (("slab", 2),), 1)
    partial_kernel = kernel_terms(padded_up, cotangent)
    grad_low = downsum(input_terms(padded_grad, kernel))
    returned = lax.all_to_all(
        grad_low.astype(jnp.bfloat16), "slab", split_axis=1, concat_axis=2, tiled=True
    ).astype(grad_low.dtype)
    total = lax.psum(partial_kernel, ("dp", "slab"))
    return (returned.astype(jnp.bfloat16), total)


def solution(mesh):
    placed = (P("dp", "slab", None, None), P("dp", None, "slab", None), P())
    return jax.shard_map(
        body,
        mesh=mesh,
        in_specs=placed,
        out_specs=(P("dp", "slab", None, None), P()),
        check_vma=False,
    )
```

profile of v0, /device:TPU:0, one launch (start us, length us, event | category | flops | bytes accessed | tf_op | source)
XLA Modules:
  0.0 253.4 jit_solution(4775696371381861457)
XLA Ops:
  7.2 0.0 copy-start
  7.2 0.0 copy-start.1
  7.2 2.2 copy.32
  9.4 6.3 %all-to-all-start.1 = ((bf16[1,64,32,128]{3,1,0,2:T(8,128)(2,1)}), bf16[1,64,32,128]{3,1,0,2:T(8,128)(2,1)}, u32[]{:S(2)}, u32[]{:S(2)}) async-start(bf16[1,64,32,128]{3,1,0,2:T(8,128)(2,1)} %copy.32), calls=%async_computation.1 | async-start | bytes 1048576 | tf_op jit(solution)/shard_map/all_to_all | solution.py:57
  15.7 1.4 fusion.14
  17.1 3.9 %collective-permute-start = (bf16[1,128,1,256]{3,2,1,0:T(2,128)(2,1)S(1)}, bf16[1,128,1,256]{3,2,1,0:T(2,128)(2,1)S(1)}, u32[]{:S(2)}, u32[]{:S(2)}) collective-permute-start(bf16[1,128,1,256]{3,2,1,0:T(2,128)(2,1)S(1)} %get-tuple-element.4), channel_id=1, source_target_pairs={{0,1},{1,2},{2,3},{4,5},{5,6},{6,7},{8,9},{9,10},{10,11},{12,13},{... | collective-permute-start | bytes 196616 | tf_op jit(solution)/shard_map/ppermute | solution.py:15
  21.0 1.3 collective-permute-start.1
  22.3 0.0 copy-done.1
  22.3 2.7 %copy.39 = bf16[1,128,16,256]{1,0,3,2:T(2,128)(2,1)} copy(bf16[1,128,16,256]{3,2,1,0:T(8,128)(2,1)S(1)} %copy-done.1) | data formatting | bytes 2097152 | tf_op args[1]
  25.0 2.1 collective-permute-done
  27.1 1.7 collective-permute-done.1
  28.8 1.1 maximum_bitcast_fusion
  29.9 1.8 copy.40
  31.7 1.6 pad.clone
  33.3 0.0 copy-start.3
  33.3 0.4 reshape.30
  33.8 0.2 copy.28
  34.0 0.0 copy-done
  34.0 0.0 copy-done.3
  34.0 3.0 %broadcast_select_fusion = f32[16,8,33,256]{3,1,2,0:T(8,128)S(1)} fusion(pred[8,33]{0,1:T(8,128)(4,1)S(1)} %copy-done.3, bf16[3,3,256,128]{3,2,1,0:T(8,128)(2,1)S(1)} %copy-done, bf16[128,18,1,7,2]{0,3,4,1,2:T(8,128)(2,1)S(1)} %slice.18, bf16[128,18,1,8,33]{0,3,4,1,2:T(8,128)(2,1)S(1)} %copy.28), kind=kOutput, calls=%fused_computation.5 | convolution fusion | flops 2496368640 | bytes 6196488 | tf_op jit(solution)/shard_map/conv_general_dilated | solution.py:46
  37.0 3.4 %copy.29 = f32[16,8,33,256]{3,0,2,1:T(8,128)} copy(f32[16,8,33,256]{3,1,2,0:T(8,128)S(1)} %broadcast_select_fusion) | data formatting | bytes 8650752 | tf_op jit(solution)/shard_map/conv_general_dilated | solution.py:46
  40.5 0.0 all-to-all-done.1
  40.5 1.4 copy.43
  41.9 0.1 copy.34
  42.0 0.0 slice-start
  42.0 0.6 copy.35
  42.5 0.7 broadcast_in_dim.10
  43.3 0.6 broadcast_in_dim.11
  43.9 0.0 slice-start.1
  43.9 0.2 broadcast_in_dim.12
  44.1 5.8 %copy.36 = bf16[1,256,16,256]{1,0,3,2:T(2,128)(2,1)} copy(bf16[1,256,16,256]{1,2,3,0:T(8,128)(2,1)S(1)} %bitcast.39) | data formatting | bytes 4194304 | tf_op jit(solution)/shard_map/broadcast_in_dim | solution.py:25
  49.9 2.3 fusion.13
  52.2 7.3 %collective-permute-start.2 = (bf16[1,256,1,256]{1,0,3,2:T(2,128)(2,1)}, bf16[1,256,1,256]{1,0,3,2:T(2,128)(2,1)}, u32[]{:S(2)}, u32[]{:S(2)}) collective-permute-start(bf16[1,256,1,256]{1,0,3,2:T(2,128)(2,1)} %get-tuple-element.2), channel_id=1, source_target_pairs={{0,1},{1,2},{2,3},{4,5},{5,6},{6,7},{8,9},{9,10},{10,11},{12,13},{... | collective-permute-start | bytes 393224 | tf_op jit(solution)/shard_map/ppermute | solution.py:15
  59.5 1.3 collective-permute-start.3
  60.8 0.0 slice-done
  60.8 0.0 slice-done.1
  60.8 2.5 slice_bitcast_fusion
  63.3 5.8 %reshape.27 = f32[256,8,2,128,2]{0,2,1,4,3:T(2,128)} reshape(f32[1,256,16,256]{1,2,3,0:T(8,128)} %slice_bitcast_fusion) | data formatting | bytes 8388608 | tf_op jit(solution)/shard_map/reshape | solution.py:30
  69.1 0.0 copy-start.2
  69.1 5.9 %reduce_sum.9 = bf16[256,8,128]{0,1,2:T(8,128)(2,1)S(1)} reduce(f32[256,8,2,128,2]{0,2,1,4,3:T(2,128)} %reshape.27, f32[]{:T(128)} %constant.0.clone.1), dimensions={2,4}, to_apply=%region_0.0 | reduce | flops 786432 | bytes 4718596 | tf_op jit(solution)/shard_map/reduce_sum | solution.py:30
  75.0 1.3 copy.30
  76.3 4.1 %all-to-all-start = ((bf16[1,256,8,128]{3,2,0,1:T(8,128)(2,1)}), bf16[1,256,8,128]{3,2,0,1:T(8,128)(2,1)}, u32[]{:S(2)}, u32[]{:S(2)}) async-start(bf16[1,256,8,128]{3,2,0,1:T(8,128)(2,1)} %copy.30), calls=%async_computation | async-start | bytes 1048576 | tf_op jit(solution)/shard_map/all_to_all | solution.py:63
  80.5 0.0 all-reduce.2.cloned.1.call-start
  80.5 0.0 collective-permute-done.2
  80.5 0.0 collective-permute-done.3
  80.6 0.0 copy-done.2
  80.6 31.0 %fusion = f32[3,3,256,128]{3,2,1,0:T(8,128)} fusion(bf16[1,128,16,256]{1,0,3,2:T(2,128)(2,1)S(1)} %copy-done.2, bf16[1,256,1,256]{1,0,3,2:T(2,128)(2,1)} %collective-permute-done.3, bf16[1,256,16,256]{1,0,3,2:T(2,128)(2,1)} %copy.36, bf16[1,256,1,256]{1,0,3,2:T(2,128)(2,1)} %collective-permute-done.2), kind=kOutput, calls=%fused_computation.1 | convolution fusion | flops 2416705536 | bytes 4587520 | tf_op jit(solution)/shard_map/conv_general_dilated | solution.py:34
  111.5 0.0 all-reduce.2.cloned.1.call-update
  111.6 0.0 all-to-all-done
  111.6 1.9 copy.44
  113.5 130.7 %all-reduce.2.cloned.1.call-done = f32[3,3,256,128]{3,2,1,0:T(8,128)} async-done(((f32[3,3,256,128]{3,2,1,0:T(8,128)}), f32[3,3,256,128]{3,2,1,0:T(8,128)}) %all-reduce.2.cloned.1.call-update) | async-done | bytes 1179664 | tf_op jit(solution)/shard_map/psum | solution.py:66
  244.2 2.4 copy.46
  (2 shorter events, 0.0 us)
Async XLA Ops:
  7.2 26.8 %copy-start = (bf16[3,3,256,128]{3,2,1,0:T(8,128)(2,1)S(1)}, bf16[3,3,256,128]{3,2,1,0:T(8,128)(2,1)}, u32[]{:S(2)}) copy-start(bf16[3,3,256,128]{3,2,1,0:T(8,128)(2,1)} %param.5) | copy-start | bytes 1769476
  7.2 15.1 %copy-start.1 = (bf16[1,128,16,256]{3,2,1,0:T(8,128)(2,1)S(1)}, bf16[1,128,16,256]{3,2,1,0:T(8,128)(2,1)}, u32[]{:S(2)}) copy-start(bf16[1,128,16,256]{3,2,1,0:T(8,128)(2,1)} %param.4) | copy-start | bytes 3145732
  9.4 31.1 %all-to-all-start.1 = ((bf16[1,64,32,128]{3,1,0,2:T(8,128)(2,1)}), bf16[1,64,32,128]{3,1,0,2:T(8,128)(2,1)}, u32[]{:S(2)}, u32[]{:S(2)}) async-start(bf16[1,64,32,128]{3,1,0,2:T(8,128)(2,1)} %copy.32), calls=%async_computation.1 | async-start | bytes 1048576 | tf_op jit(solution)/shard_map/all_to_all | solution.py:57
  17.1 10.0 %collective-permute-start = (bf16[1,128,1,256]{3,2,1,0:T(2,128)(2,1)S(1)}, bf16[1,128,1,256]{3,2,1,0:T(2,128)(2,1)S(1)}, u32[]{:S(2)}, u32[]{:S(2)}) collective-permute-start(bf16[1,128,1,256]{3,2,1,0:T(2,128)(2,1)S(1)} %get-tuple-element.4), channel_id=1, source_target_pairs={{0,1},{1,2},{2,3},{4,5},{5,6},{6,7},{8,9},{9,10},{10,11},{12,13},{... | collective-permute-start | bytes 196616 | tf_op jit(solution)/shard_map/ppermute | solution.py:15
  21.0 7.8 %collective-permute-start.1 = (bf16[1,128,1,256]{3,2,1,0:T(2,128)(2,1)S(1)}, bf16[1,128,1,256]{3,2,1,0:T(2,128)(2,1)S(1)}, u32[]{:S(2)}, u32[]{:S(2)}) collective-permute-start(bf16[1,128,1,256]{3,2,1,0:T(2,128)(2,1)S(1)} %get-tuple-element.5), channel_id=1, source_target_pairs={{1,0},{2,1},{3,2},{5,4},{6,5},{7,6},{9,8},{10,9},{11,10},{13,12},{... | collective-permute-start | bytes 196616 | tf_op jit(solution)/shard_map/ppermute | solution.py:17
  33.3 0.7 copy-start.3
  42.0 18.8 %slice-start = ((s8[4325376]{0:T(1024)(128)(4,1)}), s8[131072]{0:T(1024)(128)(4,1)S(1)}, s32[]{:S(2)}) async-start(s8[4325376]{0:T(1024)(128)(4,1)} %bitcast.36), calls=%async_computation.3 | async-start | bytes 262144
  43.9 16.9 %slice-start.1 = ((s8[4325376]{0:T(1024)(128)(4,1)}), s8[4194304]{0:T(1024)(128)(4,1)S(1)}, s32[]{:S(2)}) async-start(s8[4325376]{0:T(1024)(128)(4,1)} %bitcast.36), calls=%async_computation.4 | async-start | bytes 8388608
  52.2 28.4 %collective-permute-start.2 = (bf16[1,256,1,256]{1,0,3,2:T(2,128)(2,1)}, bf16[1,256,1,256]{1,0,3,2:T(2,128)(2,1)}, u32[]{:S(2)}, u32[]{:S(2)}) collective-permute-start(bf16[1,256,1,256]{1,0,3,2:T(2,128)(2,1)} %get-tuple-element.2), channel_id=1, source_target_pairs={{0,1},{1,2},{2,3},{4,5},{5,6},{6,7},{8,9},{9,10},{10,11},{12,13},{... | collective-permute-start | bytes 393224 | tf_op jit(solution)/shard_map/ppermute | solution.py:15
  59.5 21.0 %collective-permute-start.3 = (bf16[1,256,1,256]{1,0,3,2:T(2,128)(2,1)S(1)}, bf16[1,256,1,256]{1,0,3,2:T(2,128)(2,1)}, u32[]{:S(2)}, u32[]{:S(2)}) collective-permute-start(bf16[1,256,1,256]{1,0,3,2:T(2,128)(2,1)S(1)} %get-tuple-element.3), channel_id=1, source_target_pairs={{1,0},{2,1},{3,2},{5,4},{6,5},{7,6},{9,8},{10,9},{11,10},{13,12},{... | collective-permute-start | bytes 393224 | tf_op jit(solution)/shard_map/ppermute | solution.py:17
  69.1 11.4 %copy-start.2 = (bf16[1,128,16,256]{1,0,3,2:T(2,128)(2,1)S(1)}, bf16[1,128,16,256]{1,0,3,2:T(2,128)(2,1)}, u32[]{:S(2)}) copy-start(bf16[1,128,16,256]{1,0,3,2:T(2,128)(2,1)} %copy.39) | copy-start | bytes 3145732
  76.3 35.2 %all-to-all-start = ((bf16[1,256,8,128]{3,2,0,1:T(8,128)(2,1)}), bf16[1,256,8,128]{3,2,0,1:T(8,128)(2,1)}, u32[]{:S(2)}, u32[]{:S(2)}) async-start(bf16[1,256,8,128]{3,2,0,1:T(8,128)(2,1)} %copy.30), calls=%async_computation | async-start | bytes 1048576 | tf_op jit(solution)/shard_map/all_to_all | solution.py:63
  80.5 163.7 %all-reduce.2.cloned.1.call-start = ((), (), s32[]{:S(2)}) async-start(), calls=%async_computation.2 | async-start | bytes 2359296 | tf_op jit(solution)/shard_map/psum | solution.py:66
Sparse Core Ops, SparseCore 0:
  111.7 132.4 all-reduce.1
where the time goes:
time: 254 us; the launch traced here: 253 us
  waiting for transfers between devices  135 us (53%)
  local copies, waits for them, and re-layouts  39.3 us (15%)
  matrix products  34 us (13%)
  starting transfers between devices  24.3 us (10%)
  between operations  14.3 us (6%)
  other arithmetic  6.96 us (3%)
    psum x1, waiting for transfers between devices, body(): total = lax.psum(partial_kernel, ('dp', 'slab'))  131 us
    conv_general_dilated x1, matrix products, kernel_terms(): lax.conv_general_dilated(padded_up, grad_rows, (1, 1), ((0, 0), (1, 1)),...  31 us
    ppermute x2, starting transfers between devices, extended(): lax.ppermute(tail, axis, [(i, (i + 1) % count) for i in range(ends)])  11.3 us
    unnamed x16, local copies, waits for them, and re-layouts  9.09 us
    broadcast_in_dim x4, local copies, waits for them, and re-layouts, upsample(): return jnp.repeat(jnp.repeat(field, 2, axis=2), 2, axis=3)  7.33 us
    conv_general_dilated x5, local copies, waits for them, and re-layouts, input_terms(): lax.conv_general_dilated(padded_grad, flipped, (1, 1), ((0, 0), (1, 1)),...  6.55 us
    all_to_all x1, starting transfers between devices, body(): lax.all_to_all(images, 'slab', split_axis=2, concat_axis=1, tiled=True)  6.32 us
    reduce_sum x1, other arithmetic, downsum(): field.reshape(count, chans, rows // 2, 2, cols // 2, 2).sum(axis=(3, 5))  5.88 us
  transfers between devices with their start and end apart: 7, of which 3 were waited for; matrix products, arithmetic and copies ran while one was open for 25% of the time, Pallas kernels for 0%

commit v1 on v0

v1 whole, which is shorter than its diff:
```python
import functools

import jax
import jax.numpy as jnp
from jax import lax
from jax.experimental import pallas as pl
from jax.experimental.pallas import tpu as pltpu
from jax.sharding import PartitionSpec as P

MESH = pl.DeviceIdType.MESH
BF16 = jnp.bfloat16
F32 = jnp.float32


def each(low, high, step):
    if high - low <= 8:
        for index in range(low, high):
            step(index)
    else:
        lax.fori_loop(low, high, lambda index, carry: (step(index), carry)[1], 0)


def kernel(
    images, cotangent, weights, grad_images, grad_kernel,
    wide, rows_up, box, pairs, flat, image_send, image_all, image_wide, input_send, input_all, input_wide,
    term_send, term_all, term_sum, total,
    halo_out, halo_in, image_out, image_in, input_out, input_in, term_out, term_in, sum_out, sum_in,
    slab_out, slab_in, dp_out, dp_in,
):
    slabs, parts = lax.axis_size("slab"), lax.axis_size("dp")
    me, part = lax.axis_index("slab"), lax.axis_index("dp")
    chans, low_rows, low_cols = images.shape
    outs, rows, cols = cotangent.shape
    all_chans = chans * slabs
    taps = weights.shape[0]
    own_rows = rows // 2
    shard = term_all.shape[2]

    def slab_at(distance):
        return lax.rem(me + distance + slabs, slabs)

    def part_at(distance):
        return lax.rem(part + distance + parts, parts)

    barrier = pltpu.get_barrier_semaphore()
    each(1, slabs, lambda r: pl.semaphore_signal(barrier, inc=1, device_id={"slab": slab_at(r)}, device_id_type=MESH))
    each(1, parts, lambda j: pl.semaphore_signal(barrier, inc=1, device_id={"dp": part_at(j)}, device_id_type=MESH))

    def remote(src, dst, send, recv, device):
        return pltpu.make_async_remote_copy(
            src_ref=src, dst_ref=dst, send_sem=send, recv_sem=recv, device_id=device, device_id_type=MESH
        )

    for o in range(0, outs, 16):
        for half in range(cols // 128):
            part_of = cotangent[pl.ds(o, 16), :, pl.ds(half * 128, 128)]
            wide[half, pl.ds(o * rows, 16 * rows), :] = part_of.astype(F32).reshape(16 * rows, 128)

    def turn(row):
        for half in range(cols // 128):
            rows_up[:, pl.ds((row + 1) * cols + half * 128, 128)] = wide[
                half, pl.ds(row, outs, stride=rows), :
            ].astype(BF16)

    turn(0)
    turn(rows - 1)
    pl.semaphore_wait(barrier, slabs - 1 + parts - 1)

    first, last = pl.ds(0, cols), pl.ds((rows + 1) * cols, cols)
    head = remote(rows_up.at[:, pl.ds(cols, cols)], rows_up.at[:, last], halo_out.at[0], halo_in.at[0], {"slab": slab_at(-1)})
    tail = remote(rows_up.at[:, pl.ds(rows * cols, cols)], rows_up.at[:, first], halo_out.at[1], halo_in.at[1], {"slab": slab_at(1)})

    @pl.when(me > 0)
    def _():
        head.start()

    @pl.when(me < slabs - 1)
    def _():
        tail.start()

    image_wide[...] = images[...].astype(F32).reshape(chans * low_rows, low_cols)

    def image_block(dst, slab):
        for p in range(own_rows):
            dst[:, pl.ds(p * low_cols, low_cols)] = image_wide[
                pl.ds(slab * own_rows + p, chans, stride=low_rows), :
            ].astype(BF16)

    image_copies = [None]
    for r in range(1, slabs):
        target = slab_at(-r)
        image_block(image_send.at[r], target)
        copy = remote(image_send.at[r], image_all.at[r], image_out.at[r], image_in.at[r], {"slab": target})
        copy.start()
        image_copies.append(copy)
    image_block(image_all.at[0], me)

    for row in range(1, rows - 1):
        turn(row)

    j = lax.broadcasted_iota(jnp.int32, (cols, low_cols), 0)
    q = lax.broadcasted_iota(jnp.int32, (cols, low_cols), 1)
    for b in range(3):
        gap = j - 2 * q + b
        hit = jnp.where((gap == 1) | (gap == 2), 1.0, 0.0).astype(BF16)
        pairs[pl.ds(0, cols), pl.ds(b * low_cols, low_cols)] = hit
        pairs[pl.ds(cols, cols), pl.ds(b * low_cols, low_cols)] = hit
    for tap in range(taps):
        flat[:, pl.ds(tap * outs, outs)] = weights[tap]

    def box_row(p, a):
        start = (2 * p - a + 2) * cols
        if not isinstance(p, int):
            start = pl.multiple_of(start, 128)
        sums = jnp.dot(rows_up[:, pl.ds(start, 2 * cols)], pairs[...], preferred_element_type=F32).astype(BF16)
        at = p * low_cols
        if not isinstance(p, int):
            at = pl.multiple_of(at, 128)
        for b in range(3):
            box[pl.ds((a * 3 + b) * outs, outs), pl.ds(at, low_cols)] = sums[:, b * low_cols:(b + 1) * low_cols]

    def inner(p, carry):
        for a in range(3):
            box_row(p, a)
        return carry

    lax.fori_loop(1, own_rows - 1, inner, 0)
    box_row(0, 0)
    box_row(0, 1)
    box_row(own_rows - 1, 1)
    box_row(own_rows - 1, 2)

    @pl.when(me > 0)
    def _():
        tail.wait_recv()

    @pl.when(me == 0)
    def _():
        rows_up[:, first] = jnp.zeros((outs, cols), BF16)

    @pl.when(me < slabs - 1)
    def _():
        head.wait_recv()

    @pl.when(me == slabs - 1)
    def _():
        rows_up[:, last] = jnp.zeros((outs, cols), BF16)

    box_row(0, 2)
    box_row(own_rows - 1, 0)

    used = taps * chans
    padded = parts * shard

    def terms(r):
        product = lax.dot_general(
            image_all[r], box[...], (((1,), (1,)), ((), ())), preferred_element_type=F32
        ).astype(BF16)
        for tap in range(taps):
            term_send[r, pl.ds(tap * chans, chans), :] = product[:, tap * outs:(tap + 1) * outs]
        if padded > used:
            term_send[r, pl.ds(used, padded - used), :] = jnp.zeros((padded - used, outs), BF16)

    def term_copy(r, step):
        peer = part_at(step)
        return remote(
            term_send.at[r, pl.ds(pl.multiple_of(peer * shard, 16), shard)], term_all.at[r, step],
            term_out.at[r, step], term_in.at[r, step], {"dp": peer},
        )

    sum_copies = [None] * slabs

    def gather_terms(r):
        acc = term_send[r, pl.ds(pl.multiple_of(part * shard, 16), shard), :].astype(F32)
        each(1, parts, lambda step: term_copy(r, step).wait_recv())
        if parts <= 8:
            for step in range(1, parts):
                acc = acc + term_all[r, step].astype(F32)
        else:
            acc = lax.fori_loop(1, parts, lambda step, value: value + term_all[r, step].astype(F32), acc)
        if r == 0:
            term_sum[0, 0] = acc
        else:
            term_sum[1, r] = acc
            copy = remote(term_sum.at[1, r], term_sum.at[0, r], sum_out.at[r], sum_in.at[r], {"slab": slab_at(r)})
            copy.start()
            sum_copies[r] = copy

    terms(0)
    each(1, parts, lambda step: term_copy(0, step).start())

    tile = 2 * low_cols
    for n in range(own_rows * low_cols // tile):
        at = pl.ds(n * tile, tile)
        input_send[:, at] = jnp.dot(flat[...], box[:, at], preferred_element_type=F32).astype(BF16)

    input_copies = [None]
    for r in range(1, slabs):
        image_copies[r].wait_recv()
        terms(r)
        each(1, parts, lambda step: term_copy(r, step).start())
        image_copies[r].wait_send()
        target = slab_at(-r)
        copy = remote(
            input_send.at[pl.ds(pl.multiple_of(target * chans, 16), chans)], input_all.at[me],
            input_out.at[r], input_in.at[r], {"slab": target},
        )
        copy.start()
        input_copies.append(copy)
        gather_terms(r - 1)
    gather_terms(slabs - 1)
    input_all[me] = input_send[pl.ds(pl.multiple_of(me * chans, 16), chans), :]

    for r in range(1, slabs):
        sum_copies[r].wait_recv()
    mine = pl.ds(pl.multiple_of(part * shard, 16), shard)
    total[me, mine, :] = functools.reduce(lambda x, y: x + y, [term_sum[0, r] for r in range(slabs)]).astype(BF16)

    slab_copies = [None]
    for r in range(1, slabs):
        copy = remote(total.at[me, mine], total.at[me, mine], slab_out.at[r], slab_in.at[r], {"slab": slab_at(r)})
        copy.start()
        slab_copies.append(copy)

    def dp_copy(r, step):
        source = slab_at(-r)
        return remote(total.at[source, mine], total.at[source, mine], dp_out.at[r, step], dp_in.at[r, step], {"dp": part_at(step)})

    each(1, parts, lambda step: dp_copy(0, step).start())
    for r in range(1, slabs):
        slab_copies[r].wait_recv()
        each(1, parts, lambda step: dp_copy(r, step).start())

    for r in range(1, slabs):
        input_copies[r].wait_recv()
    for s in range(slabs):
        for p in range(own_rows):
            input_wide[pl.ds(s * own_rows + p, chans, stride=low_rows), :] = input_all[
                s, :, pl.ds(p * low_cols, low_cols)
            ].astype(F32)
    grad_images[...] = input_wide[...].astype(BF16).reshape(chans, low_rows, low_cols)

    for r in range(slabs):
        each(1, parts, lambda step: dp_copy(r, step).wait_recv())
    for s in range(slabs):
        for tap in range(taps):
            grad_kernel[tap, pl.ds(s * chans, chans), :] = total[s, pl.ds(tap * chans, chans), :].astype(F32)

    @pl.when(me > 0)
    def _():
        head.wait_send()

    @pl.when(me < slabs - 1)
    def _():
        tail.wait_send()

    for r in range(1, slabs):
        input_copies[r].wait_send()
        sum_copies[r].wait_send()
        slab_copies[r].wait_send()
    for r in range(slabs):
        each(1, parts, lambda step: term_copy(r, step).wait_send())
        each(1, parts, lambda step: dp_copy(r, step).wait_send())


def body(images, cotangent, weights):
    slabs, parts = lax.axis_size("slab"), lax.axis_size("dp")
    _, chans, low_rows, low_cols = images.shape
    _, outs, rows, cols = cotangent.shape
    height, width, all_chans, _ = weights.shape
    taps = height * width
    own_rows = rows // 2
    area = own_rows * low_cols
    shard = -(-(taps * chans) // (parts * 16)) * 16
    dma = pltpu.SemaphoreType.DMA
    vmem = pl.BlockSpec(memory_space=pltpu.VMEM)
    grad_images, grad_kernel = pl.pallas_call(
        kernel,
        out_shape=(
            jax.ShapeDtypeStruct((chans, low_rows, low_cols), BF16),
            jax.ShapeDtypeStruct((taps, all_chans, outs), F32),
        ),
        in_specs=[vmem] * 3,
        out_specs=(vmem, vmem),
        scratch_shapes=[
            pltpu.VMEM((cols // 128, outs * rows, 128), F32),
            pltpu.VMEM((outs, (rows + 2) * cols), BF16),
            pltpu.VMEM((taps * outs, area), BF16),
            pltpu.VMEM((2 * cols, 3 * low_cols), BF16),
            pltpu.VMEM((all_chans, taps * outs), BF16),
            pltpu.VMEM((slabs, chans, area), BF16),
            pltpu.VMEM((slabs, chans, area), BF16),
            pltpu.VMEM((chans * low_rows, low_cols), F32),
            pltpu.VMEM((all_chans, area), BF16),
            pltpu.VMEM((slabs, chans, area), BF16),
            pltpu.VMEM((chans * low_rows, low_cols), F32),
            pltpu.VMEM((slabs, parts * shard, outs), BF16),
            pltpu.VMEM((slabs, parts, shard, outs), BF16),
            pltpu.VMEM((2, slabs, shard, outs), F32),
            pltpu.VMEM((slabs, parts * shard, outs), BF16),
            dma((2,)), dma((2,)), dma((slabs,)), dma((slabs,)), dma((slabs,)), dma((slabs,)),
            dma((slabs, parts)), dma((slabs, parts)), dma((slabs,)), dma((slabs,)),
            dma((slabs,)), dma((slabs,)), dma((slabs, parts)), dma((slabs, parts)),
        ],
        compiler_params=pltpu.CompilerParams(
            collective_id=0, has_side_effects=True, vmem_limit_bytes=48 * 1024 * 1024
        ),
    )(images[0], cotangent[0], weights.reshape(taps, all_chans, outs))
    return grad_images[None], grad_kernel.reshape(weights.shape)


def solution(mesh):
    placed = (P("dp", "slab", None, None), P("dp", None, "slab", None), P())
    return jax.shard_map(
        body,
        mesh=mesh,
        in_specs=placed,
        out_specs=(P("dp", "slab", None, None), P()),
        check_vma=False,
    )
```

time: 254 us -> 51.2 us (0.20)
  waiting for transfers between devices: 135 us -> 0 us
  Pallas kernels: 0 us -> 45.2 us
  local copies, waits for them, and re-layouts: 39.3 us -> 5.13 us
  matrix products: 34 us -> 0 us
  starting transfers between devices: 24.3 us -> 0 us
  between operations: 14.3 us -> 0.65 us
  other arithmetic: 6.96 us -> 0 us
    psum x1 -> x0, waiting for transfers between devices: 131 us -> none  [body(): total = lax.psum(partial_kernel, ('dp', 'slab'))]
    pallas_call x0 -> x1, Pallas kernels: none -> 45.2 us  [body(): pl.pallas_call(kernel, out_shape=(jax.ShapeDtypeStruct((chans, low_rows,...]
    conv_general_dilated x2 -> x0, matrix products: 34 us -> none  [the longest x1 31 us: kernel_terms(): lax.conv_general_dilated(padded_up, grad_rows, (1, 1), ((0, 0), (1, 1)),...]
    ppermute x4 -> x0, starting transfers between devices: 13.8 us -> none  [the longest x2 11.3 us: extended(): lax.ppermute(tail, axis, [(i, (i + 1) % count) for i in range(ends)])]
    all_to_all x2 -> x0, starting transfers between devices: 10.5 us -> none  [the longest x1 6.32 us: body(): lax.all_to_all(images, 'slab', split_axis=2, concat_axis=1, tiled=True)]
    broadcast_in_dim x4 -> x0, local copies, waits for them, and re-layouts: 7.33 us -> none  [upsample(): return jnp.repeat(jnp.repeat(field, 2, axis=2), 2, axis=3)]
    conv_general_dilated x5 -> x0, local copies, waits for them, and re-layouts: 6.55 us -> none  [input_terms(): lax.conv_general_dilated(padded_grad, flipped, (1, 1), ((0, 0), (1, 1)),...]
    reduce_sum x1 -> x0, other arithmetic: 5.88 us -> none  [downsum(): field.reshape(count, chans, rows // 2, 2, cols // 2, 2).sum(axis=(3, 5))]
  transfers between devices with their start and end apart: 7 -> 0, of which waited for: 3 -> 0; matrix products, arithmetic and copies ran while one was open for 25% -> 0% of each run, Pallas kernels for 0% -> 0%
where the time goes in v1:
time: 51.2 us; the launch traced here: 51 us
  Pallas kernels  45.2 us (88%)
  local copies, waits for them, and re-layouts  5.13 us (10%)
  between operations  0.65 us (1%)
    pallas_call x1, Pallas kernels, body(): pl.pallas_call(kernel, out_shape=(jax.ShapeDtypeStruct((chans, low_rows,...  45.2 us
    unnamed x8, local copies, waits for them, and re-layouts  5.13 us

profile of v1, /device:TPU:0, one launch (start us, length us, event | category | flops | bytes accessed | tf_op | source)
XLA Modules:
  0.0 51.0 jit_solution(3885215266368059362)
XLA Ops:
  0.6 0.0 copy-start
  0.6 1.2 %copy-done = bf16[1,128,16,256]{3,2,1,0:T(8,128)(2,1)S(1)} copy-done((bf16[1,128,16,256]{3,2,1,0:T(8,128)(2,1)S(1)}, bf16[1,128,16,256]{3,2,1,0:T(8,128)(2,1)}, u32[]{:S(2)}) %copy-start) | copy-done | bytes 1048600
  1.9 0.0 copy-start.1
  1.9 1.1 %copy-done.1 = bf16[3,3,256,128]{3,2,1,0:T(8,128)(2,1)S(1)} copy-done((bf16[3,3,256,128]{3,2,1,0:T(8,128)(2,1)S(1)}, bf16[3,3,256,128]{3,2,1,0:T(8,128)(2,1)}, u32[]{:S(2)}) %copy-start.1) | copy-done | bytes 589848
  2.9 0.0 copy-start.2
  2.9 1.0 %copy-done.2 = bf16[1,64,32,128]{3,2,1,0:T(8,128)(2,1)S(1)} copy-done((bf16[1,64,32,128]{3,2,1,0:T(8,128)(2,1)S(1)}, bf16[1,64,32,128]{3,2,1,0:T(8,128)(2,1)}, u32[]{:S(2)}) %copy-start.2) | copy-done | bytes 524312
  4.0 45.2 %shard_map.50 = (bf16[64,32,128]{2,1,0:T(8,128)(2,1)S(1)}, f32[9,256,128]{2,1,0:T(8,128)S(1)}) custom-call(bf16[64,32,128]{2,1,0:T(8,128)(2,1)S(1)} %bitcast.9, bf16[128,16,256]{2,1,0:T(8,128)(2,1)S(1)} %bitcast.6, bf16[9,256,128]{2,1,0:T(8,128)(2,1)S(1)} %bitcast.7), custom_call_target="tpu_custom_call" | custom-call | tf_op jit(solution)/shard_map/pallas_call | solution.py:277
  49.2 0.8 %copy.7 = bf16[1,64,32,128]{3,2,1,0:T(8,128)(2,1)} copy(bf16[1,64,32,128]{3,2,1,0:T(8,128)(2,1)S(1)} %bitcast.8) | data formatting | bytes 1048576
  50.0 1.0 %copy.8 = f32[3,3,256,128]{3,2,1,0:T(8,128)} copy(f32[3,3,256,128]{3,2,1,0:T(8,128)S(1)} %bitcast.5) | data formatting | bytes 2359296
Async XLA Ops:
  0.6 1.2 %copy-start = (bf16[1,128,16,256]{3,2,1,0:T(8,128)(2,1)S(1)}, bf16[1,128,16,256]{3,2,1,0:T(8,128)(2,1)}, u32[]{:S(2)}) copy-start(bf16[1,128,16,256]{3,2,1,0:T(8,128)(2,1)} %param.4) | copy-start | bytes 3145732
  1.9 1.1 %copy-start.1 = (bf16[3,3,256,128]{3,2,1,0:T(8,128)(2,1)S(1)}, bf16[3,3,256,128]{3,2,1,0:T(8,128)(2,1)}, u32[]{:S(2)}) copy-start(bf16[3,3,256,128]{3,2,1,0:T(8,128)(2,1)} %param.5) | copy-start | bytes 1769476
  2.9 1.0 %copy-start.2 = (bf16[1,64,32,128]{3,2,1,0:T(8,128)(2,1)S(1)}, bf16[1,64,32,128]{3,2,1,0:T(8,128)(2,1)}, u32[]{:S(2)}) copy-start(bf16[1,64,32,128]{3,2,1,0:T(8,128)(2,1)} %param.3) | copy-start | bytes 1572868

commit v2 on v1

--- a/solution.py
+++ b/solution.py
@@ -21,11 +21,11 @@
 
 
 def kernel(
-    images, cotangent, weights, grad_images, grad_kernel,
-    wide, rows_up, box, pairs, flat, image_send, image_all, image_wide, input_send, input_all, input_wide,
+    images_from, cotangent_from, weights_from, grad_images, grad_kernel,
+    images, cotangent, weights, loads, wide, rows_up, box, pairs, flat, image_send, image_all, image_wide, input_send, input_all, input_wide,
     term_send, term_all, term_sum, total,
     halo_out, halo_in, image_out, image_in, input_out, input_in, term_out, term_in, sum_out, sum_in,
-    slab_out, slab_in, dp_out, dp_in,
+    slab_out, slab_in, dp_out, dp_in, core_out, core_in,
 ):
     slabs, parts = lax.axis_size("slab"), lax.axis_size("dp")
     me, part = lax.axis_index("slab"), lax.axis_index("dp")
@@ -35,12 +35,22 @@
     taps = weights.shape[0]
     own_rows = rows // 2
     shard = term_all.shape[2]
+    cores = core_out.shape[2]
+    chips = parts // cores
+    core = lax.rem(part, cores)
 
     def slab_at(distance):
         return lax.rem(me + distance + slabs, slabs)
 
     def part_at(distance):
         return lax.rem(part + distance + parts, parts)
+
+    load_images = pltpu.make_async_copy(images_from, images, loads.at[0])
+    load_cotangent = pltpu.make_async_copy(cotangent_from, cotangent, loads.at[1])
+    load_weights = pltpu.make_async_copy(weights_from, weights, loads.at[2])
+    load_images.start()
+    load_cotangent.start()
+    load_weights.start()
 
     barrier = pltpu.get_barrier_semaphore()
     each(1, slabs, lambda r: pl.semaphore_signal(barrier, inc=1, device_id={"slab": slab_at(r)}, device_id_type=MESH))
@@ -51,6 +61,26 @@
             src_ref=src, dst_ref=dst, send_sem=send, recv_sem=recv, device_id=device, device_id_type=MESH
         )
 
+    load_images.wait()
+    image_wide[...] = images[...].astype(F32).reshape(chans * low_rows, low_cols)
+
+    def image_block(dst, slab):
+        for p in range(own_rows):
+            dst[:, pl.ds(p * low_cols, low_cols)] = image_wide[
+                pl.ds(slab * own_rows + p, chans, stride=low_rows), :
+            ].astype(BF16)
+
+    image_copies = [None]
+    for r in range(1, slabs):
+        target = slab_at(-r)
+        image_block(image_send.at[r], target)
+        if r == 1:
+            pl.semaphore_wait(barrier, slabs - 1 + parts - 1)
+        copy = remote(image_send.at[r], image_all.at[r], image_out.at[r], image_in.at[r], {"slab": target})
+        copy.start()
+        image_copies.append(copy)
+
+    load_cotangent.wait()
     for o in range(0, outs, 16):
         for half in range(cols // 128):
             part_of = cotangent[pl.ds(o, 16), :, pl.ds(half * 128, 128)]
@@ -64,7 +94,6 @@
 
     turn(0)
     turn(rows - 1)
-    pl.semaphore_wait(barrier, slabs - 1 + parts - 1)
 
     first, last = pl.ds(0, cols), pl.ds((rows + 1) * cols, cols)
     head = remote(rows_up.at[:, pl.ds(cols, cols)], rows_up.at[:, last], halo_out.at[0], halo_in.at[0], {"slab": slab_at(-1)})
@@ -78,21 +107,6 @@
     def _():
         tail.start()
 
-    image_wide[...] = images[...].astype(F32).reshape(chans * low_rows, low_cols)
-
-    def image_block(dst, slab):
-        for p in range(own_rows):
-            dst[:, pl.ds(p * low_cols, low_cols)] = image_wide[
-                pl.ds(slab * own_rows + p, chans, stride=low_rows), :
-            ].astype(BF16)
-
-    image_copies = [None]
-    for r in range(1, slabs):
-        target = slab_at(-r)
-        image_block(image_send.at[r], target)
-        copy = remote(image_send.at[r], image_all.at[r], image_out.at[r], image_in.at[r], {"slab": target})
-        copy.start()
-        image_copies.append(copy)
     image_block(image_all.at[0], me)
 
     for row in range(1, rows - 1):
@@ -105,6 +119,7 @@
         hit = jnp.where((gap == 1) | (gap == 2), 1.0, 0.0).astype(BF16)
         pairs[pl.ds(0, cols), pl.ds(b * low_cols, low_cols)] = hit
         pairs[pl.ds(cols, cols), pl.ds(b * low_cols, low_cols)] = hit
+    load_weights.wait()
     for tap in range(taps):
         flat[:, pl.ds(tap * outs, outs)] = weights[tap]
 
@@ -196,9 +211,6 @@
 
     input_copies = [None]
     for r in range(1, slabs):
-        image_copies[r].wait_recv()
-        terms(r)
-        each(1, parts, lambda step: term_copy(r, step).start())
         image_copies[r].wait_send()
         target = slab_at(-r)
         copy = remote(
@@ -207,6 +219,9 @@
         )
         copy.start()
         input_copies.append(copy)
+        image_copies[r].wait_recv()
+        terms(r)
+        each(1, parts, lambda step: term_copy(r, step).start())
         gather_terms(r - 1)
     gather_terms(slabs - 1)
     input_all[me] = input_send[pl.ds(pl.multiple_of(me * chans, 16), chans), :]
@@ -224,12 +239,32 @@
 
     def dp_copy(r, step):
         source = slab_at(-r)
-        return remote(total.at[source, mine], total.at[source, mine], dp_out.at[r, step], dp_in.at[r, step], {"dp": part_at(step)})
-
-    each(1, parts, lambda step: dp_copy(0, step).start())
-    for r in range(1, slabs):
-        slab_copies[r].wait_recv()
-        each(1, parts, lambda step: dp_copy(r, step).start())
+        return remote(total.at[source, mine], total.at[source, mine], dp_out.at[r, step], dp_in.at[r, step], {"dp": part_at(step * cores)})
+
+    def core_copy(r, step, other):
+        source = slab_at(-r)
+        at = pl.ds(pl.multiple_of(part_at(-step * cores) * shard, 16), shard)
+        device = part - core + lax.rem(core + other, cores)
+        return remote(
+            total.at[source, at], total.at[source, at], core_out.at[r, step, other], core_in.at[r, step, other], {"dp": device}
+        )
+
+    def for_cores(r, step, act):
+        for other in range(1, cores):
+            act(core_copy(r, step, other))
+
+    for r in range(slabs):
+        if r:
+            slab_copies[r].wait_recv()
+        each(1, chips, lambda step: dp_copy(r, step).start())
+        for_cores(r, 0, lambda copy: copy.start())
+
+    def forward(r, step):
+        dp_copy(r, step).wait_recv()
+        for_cores(r, step, lambda copy: copy.start())
+
+    for r in range(slabs):
+        each(1, chips, lambda step: forward(r, step))
 
     for r in range(1, slabs):
         input_copies[r].wait_recv()
@@ -241,7 +276,7 @@
     grad_images[...] = input_wide[...].astype(BF16).reshape(chans, low_rows, low_cols)
 
     for r in range(slabs):
-        each(1, parts, lambda step: dp_copy(r, step).wait_recv())
+        each(0, chips, lambda step: for_cores(r, step, lambda copy: copy.wait_recv()))
     for s in range(slabs):
         for tap in range(taps):
             grad_kernel[tap, pl.ds(s * chans, chans), :] = total[s, pl.ds(tap * chans, chans), :].astype(F32)
@@ -260,7 +295,8 @@
         slab_copies[r].wait_send()
     for r in range(slabs):
         each(1, parts, lambda step: term_copy(r, step).wait_send())
-        each(1, parts, lambda step: dp_copy(r, step).wait_send())
+        each(1, chips, lambda step: dp_copy(r, step).wait_send())
+        each(0, chips, lambda step: for_cores(r, step, lambda copy: copy.wait_send()))
 
 
 def body(images, cotangent, weights):
@@ -272,6 +308,8 @@
     own_rows = rows // 2
     area = own_rows * low_cols
     shard = -(-(taps * chans) // (parts * 16)) * 16
+    cores = 2 if parts % 2 == 0 else 1
+    chips = parts // cores
     dma = pltpu.SemaphoreType.DMA
     vmem = pl.BlockSpec(memory_space=pltpu.VMEM)
     grad_images, grad_kernel = pl.pallas_call(
@@ -280,9 +318,13 @@
             jax.ShapeDtypeStruct((chans, low_rows, low_cols), BF16),
             jax.ShapeDtypeStruct((taps, all_chans, outs), F32),
         ),
-        in_specs=[vmem] * 3,
+        in_specs=[pl.BlockSpec(memory_space=pltpu.HBM)] * 3,
         out_specs=(vmem, vmem),
         scratch_shapes=[
+            pltpu.VMEM((chans, low_rows, low_cols), BF16),
+            pltpu.VMEM((outs, rows, cols), BF16),
+            pltpu.VMEM((taps, all_chans, outs), BF16),
+            dma((3,)),
             pltpu.VMEM((cols // 128, outs * rows, 128), F32),
             pltpu.VMEM((outs, (rows + 2) * cols), BF16),
             pltpu.VMEM((taps * outs, area), BF16),
@@ -300,7 +342,8 @@
             pltpu.VMEM((slabs, parts * shard, outs), BF16),
             dma((2,)), dma((2,)), dma((slabs,)), dma((slabs,)), dma((slabs,)), dma((slabs,)),
             dma((slabs, parts)), dma((slabs, parts)), dma((slabs,)), dma((slabs,)),
-            dma((slabs,)), dma((slabs,)), dma((slabs, parts)), dma((slabs, parts)),
+            dma((slabs,)), dma((slabs,)), dma((slabs, chips)), dma((slabs, chips)),
+            dma((slabs, chips, cores)), dma((slabs, chips, cores)),
         ],
         compiler_params=pltpu.CompilerParams(
             collective_id=0, has_side_effects=True, vmem_limit_bytes=48 * 1024 * 1024

time: 51.2 us -> 56.1 us (1.096)
  Pallas kernels: 45.2 us -> 50.1 us
    pallas_call x1, Pallas kernels: 45.2 us -> 50.1 us  [body(): pl.pallas_call(kernel, out_shape=(jax.ShapeDtypeStruct((chans, low_rows,...]
where the time goes in v2:
time: 56.1 us; the launch traced here: 55.9 us
  Pallas kernels  50.1 us (89%)
  local copies, waits for them, and re-layouts  5.13 us (9%)
  between operations  0.65 us (1%)
    pallas_call x1, Pallas kernels, body(): pl.pallas_call(kernel, out_shape=(jax.ShapeDtypeStruct((chans, low_rows,...  50.1 us
    unnamed x8, local copies, waits for them, and re-layouts  5.13 us

profile of v2, /device:TPU:0, one launch (start us, length us, event | category | flops | bytes accessed | tf_op | source)
XLA Modules:
  0.0 55.9 jit_solution(16996749018085584786)
XLA Ops:
  0.6 0.0 copy-start
  0.6 1.2 %copy-done = bf16[1,128,16,256]{3,2,1,0:T(8,128)(2,1)S(1)} copy-done((bf16[1,128,16,256]{3,2,1,0:T(8,128)(2,1)S(1)}, bf16[1,128,16,256]{3,2,1,0:T(8,128)(2,1)}, u32[]{:S(2)}) %copy-start) | copy-done | bytes 1048600
  1.9 0.0 copy-start.1
  1.9 1.1 %copy-done.1 = bf16[3,3,256,128]{3,2,1,0:T(8,128)(2,1)S(1)} copy-done((bf16[3,3,256,128]{3,2,1,0:T(8,128)(2,1)S(1)}, bf16[3,3,256,128]{3,2,1,0:T(8,128)(2,1)}, u32[]{:S(2)}) %copy-start.1) | copy-done | bytes 589848
  2.9 0.0 copy-start.2
  2.9 1.0 %copy-done.2 = bf16[1,64,32,128]{3,2,1,0:T(8,128)(2,1)S(1)} copy-done((bf16[1,64,32,128]{3,2,1,0:T(8,128)(2,1)S(1)}, bf16[1,64,32,128]{3,2,1,0:T(8,128)(2,1)}, u32[]{:S(2)}) %copy-start.2) | copy-done | bytes 524312
  4.0 50.1 %shard_map.50 = (bf16[64,32,128]{2,1,0:T(8,128)(2,1)S(1)}, f32[9,256,128]{2,1,0:T(8,128)S(1)}) custom-call(bf16[64,32,128]{2,1,0:T(8,128)(2,1)S(1)} %bitcast.9, bf16[128,16,256]{2,1,0:T(8,128)(2,1)S(1)} %bitcast.6, bf16[9,256,128]{2,1,0:T(8,128)(2,1)S(1)} %bitcast.7), custom_call_target="tpu_custom_call" | custom-call | tf_op jit(solution)/shard_map/pallas_call | solution.py:315
  54.1 0.8 %copy.7 = bf16[1,64,32,128]{3,2,1,0:T(8,128)(2,1)} copy(bf16[1,64,32,128]{3,2,1,0:T(8,128)(2,1)S(1)} %bitcast.8) | data formatting | bytes 1048576
  54.9 1.0 %copy.8 = f32[3,3,256,128]{3,2,1,0:T(8,128)} copy(f32[3,3,256,128]{3,2,1,0:T(8,128)S(1)} %bitcast.5) | data formatting | bytes 2359296
Async XLA Ops:
  0.6 1.2 %copy-start = (bf16[1,128,16,256]{3,2,1,0:T(8,128)(2,1)S(1)}, bf16[1,128,16,256]{3,2,1,0:T(8,128)(2,1)}, u32[]{:S(2)}) copy-start(bf16[1,128,16,256]{3,2,1,0:T(8,128)(2,1)} %param.4) | copy-start | bytes 3145732
  1.9 1.1 %copy-start.1 = (bf16[3,3,256,128]{3,2,1,0:T(8,128)(2,1)S(1)}, bf16[3,3,256,128]{3,2,1,0:T(8,128)(2,1)}, u32[]{:S(2)}) copy-start(bf16[3,3,256,128]{3,2,1,0:T(8,128)(2,1)} %param.5) | copy-start | bytes 1769476
  2.9 1.0 %copy-start.2 = (bf16[1,64,32,128]{3,2,1,0:T(8,128)(2,1)S(1)}, bf16[1,64,32,128]{3,2,1,0:T(8,128)(2,1)}, u32[]{:S(2)}) copy-start(bf16[1,64,32,128]{3,2,1,0:T(8,128)(2,1)} %param.3) | copy-start | bytes 1572868

commit v3 on v2

--- a/solution.py
+++ b/solution.py
@@ -21,8 +21,8 @@
 
 
 def kernel(
-    images_from, cotangent_from, weights_from, grad_images, grad_kernel,
-    images, cotangent, weights, loads, wide, rows_up, box, pairs, flat, image_send, image_all, image_wide, input_send, input_all, input_wide,
+    images, cotangent, weights, grad_images, grad_kernel,
+    wide, rows_up, box, pairs, flat, image_send, image_all, image_wide, input_send, input_all, input_wide,
     term_send, term_all, term_sum, total,
     halo_out, halo_in, image_out, image_in, input_out, input_in, term_out, term_in, sum_out, sum_in,
     slab_out, slab_in, dp_out, dp_in, core_out, core_in,
@@ -45,13 +45,6 @@
     def part_at(distance):
         return lax.rem(part + distance + parts, parts)
 
-    load_images = pltpu.make_async_copy(images_from, images, loads.at[0])
-    load_cotangent = pltpu.make_async_copy(cotangent_from, cotangent, loads.at[1])
-    load_weights = pltpu.make_async_copy(weights_from, weights, loads.at[2])
-    load_images.start()
-    load_cotangent.start()
-    load_weights.start()
-
     barrier = pltpu.get_barrier_semaphore()
     each(1, slabs, lambda r: pl.semaphore_signal(barrier, inc=1, device_id={"slab": slab_at(r)}, device_id_type=MESH))
     each(1, parts, lambda j: pl.semaphore_signal(barrier, inc=1, device_id={"dp": part_at(j)}, device_id_type=MESH))
@@ -61,7 +54,20 @@
             src_ref=src, dst_ref=dst, send_sem=send, recv_sem=recv, device_id=device, device_id_type=MESH
         )
 
-    load_images.wait()
+    for o in range(0, outs, 16):
+        for half in range(cols // 128):
+            part_of = cotangent[pl.ds(o, 16), :, pl.ds(half * 128, 128)]
+            wide[half, pl.ds(o * rows, 16 * rows), :] = part_of.astype(F32).reshape(16 * rows, 128)
+
+    def turn(row):
+        for half in range(cols // 128):
+            rows_up[:, pl.ds((row + 1) * cols + half * 128, 128)] = wide[
+                half, pl.ds(row, outs, stride=rows), :
+            ].astype(BF16)
+
+    turn(0)
+    turn(rows - 1)
+
     image_wide[...] = images[...].astype(F32).reshape(chans * low_rows, low_cols)
 
     def image_block(dst, slab):
@@ -74,26 +80,9 @@
     for r in range(1, slabs):
         target = slab_at(-r)
         image_block(image_send.at[r], target)
-        if r == 1:
-            pl.semaphore_wait(barrier, slabs - 1 + parts - 1)
-        copy = remote(image_send.at[r], image_all.at[r], image_out.at[r], image_in.at[r], {"slab": target})
-        copy.start()
-        image_copies.append(copy)
-
-    load_cotangent.wait()
-    for o in range(0, outs, 16):
-        for half in range(cols // 128):
-            part_of = cotangent[pl.ds(o, 16), :, pl.ds(half * 128, 128)]
-            wide[half, pl.ds(o * rows, 16 * rows), :] = part_of.astype(F32).reshape(16 * rows, 128)
-
-    def turn(row):
-        for half in range(cols // 128):
-            rows_up[:, pl.ds((row + 1) * cols + half * 128, 128)] = wide[
-                half, pl.ds(row, outs, stride=rows), :
-            ].astype(BF16)
-
-    turn(0)
-    turn(rows - 1)
+        image_copies.append(remote(image_send.at[r], image_all.at[r], image_out.at[r], image_in.at[r], {"slab": target}))
+
+    pl.semaphore_wait(barrier, slabs - 1 + parts - 1)
 
     first, last = pl.ds(0, cols), pl.ds((rows + 1) * cols, cols)
     head = remote(rows_up.at[:, pl.ds(cols, cols)], rows_up.at[:, last], halo_out.at[0], halo_in.at[0], {"slab": slab_at(-1)})
@@ -107,6 +96,8 @@
     def _():
         tail.start()
 
+    for r in range(1, slabs):
+        image_copies[r].start()
     image_block(image_all.at[0], me)
 
     for row in range(1, rows - 1):
@@ -119,31 +110,22 @@
         hit = jnp.where((gap == 1) | (gap == 2), 1.0, 0.0).astype(BF16)
         pairs[pl.ds(0, cols), pl.ds(b * low_cols, low_cols)] = hit
         pairs[pl.ds(cols, cols), pl.ds(b * low_cols, low_cols)] = hit
-    load_weights.wait()
     for tap in range(taps):
         flat[:, pl.ds(tap * outs, outs)] = weights[tap]
 
-    def box_row(p, a):
-        start = (2 * p - a + 2) * cols
-        if not isinstance(p, int):
-            start = pl.multiple_of(start, 128)
-        sums = jnp.dot(rows_up[:, pl.ds(start, 2 * cols)], pairs[...], preferred_element_type=F32).astype(BF16)
-        at = p * low_cols
-        if not isinstance(p, int):
-            at = pl.multiple_of(at, 128)
-        for b in range(3):
-            box[pl.ds((a * 3 + b) * outs, outs), pl.ds(at, low_cols)] = sums[:, b * low_cols:(b + 1) * low_cols]
-
-    def inner(p, carry):
-        for a in range(3):
-            box_row(p, a)
-        return carry
-
-    lax.fori_loop(1, own_rows - 1, inner, 0)
-    box_row(0, 0)
-    box_row(0, 1)
-    box_row(own_rows - 1, 1)
-    box_row(own_rows - 1, 2)
+    def box_rows(places):
+        around = [rows_up[:, pl.ds((2 * p - a + 2) * cols, 2 * cols)] for p, a in places]
+        sums = jnp.dot(jnp.concatenate(around, axis=0), pairs[...], preferred_element_type=F32).astype(BF16)
+        for n, (p, a) in enumerate(places):
+            for b in range(3):
+                box[pl.ds((a * 3 + b) * outs, outs), pl.ds(p * low_cols, low_cols)] = sums[
+                    n * outs:(n + 1) * outs, b * low_cols:(b + 1) * low_cols
+                ]
+
+    edge = [(0, 2), (own_rows - 1, 0)]
+    inner = [(p, a) for a in range(3) for p in range(own_rows) if (p, a) not in edge]
+    for n in range(0, len(inner), 4):
+        box_rows(inner[n:n + 4])
 
     @pl.when(me > 0)
     def _():
@@ -161,8 +143,7 @@
     def _():
         rows_up[:, last] = jnp.zeros((outs, cols), BF16)
 
-    box_row(0, 2)
-    box_row(own_rows - 1, 0)
+    box_rows(edge)
 
     used = taps * chans
     padded = parts * shard
@@ -211,6 +192,10 @@
 
     input_copies = [None]
     for r in range(1, slabs):
+        image_copies[r].wait_recv()
+        terms(r)
+        each(1, parts, lambda step: term_copy(r, step).start())
+        gather_terms(r - 1)
         image_copies[r].wait_send()
         target = slab_at(-r)
         copy = remote(
@@ -219,10 +204,6 @@
         )
         copy.start()
         input_copies.append(copy)
-        image_copies[r].wait_recv()
-        terms(r)
-        each(1, parts, lambda step: term_copy(r, step).start())
-        gather_terms(r - 1)
     gather_terms(slabs - 1)
     input_all[me] = input_send[pl.ds(pl.multiple_of(me * chans, 16), chans), :]
 
@@ -318,13 +299,9 @@
             jax.ShapeDtypeStruct((chans, low_rows, low_cols), BF16),
             jax.ShapeDtypeStruct((taps, all_chans, outs), F32),
         ),
-        in_specs=[pl.BlockSpec(memory_space=pltpu.HBM)] * 3,
+        in_specs=[vmem] * 3,
         out_specs=(vmem, vmem),
         scratch_shapes=[
-            pltpu.VMEM((chans, low_rows, low_cols), BF16),
-            pltpu.VMEM((outs, rows, cols), BF16),
-            pltpu.VMEM((taps, all_chans, outs), BF16),
-            dma((3,)),
             pltpu.VMEM((cols // 128, outs * rows, 128), F32),
             pltpu.VMEM((outs, (rows + 2) * cols), BF16),
             pltpu.VMEM((taps * outs, area), BF16),

time: 56.1 us -> 51.3 us (0.914)
  Pallas kernels: 50.1 us -> 45.3 us
    pallas_call x1, Pallas kernels: 50.1 us -> 45.3 us  [body(): pl.pallas_call(kernel, out_shape=(jax.ShapeDtypeStruct((chans, low_rows,...]
where the time goes in v3:
time: 51.3 us; the launch traced here: 51.1 us
  Pallas kernels  45.3 us (88%)
  local copies, waits for them, and re-layouts  5.13 us (10%)
  between operations  0.65 us (1%)
    pallas_call x1, Pallas kernels, body(): pl.pallas_call(kernel, out_shape=(jax.ShapeDtypeStruct((chans, low_rows,...  45.3 us
    unnamed x8, local copies, waits for them, and re-layouts  5.13 us

profile of v3, /device:TPU:0, one launch (start us, length us, event | category | flops | bytes accessed | tf_op | source)
XLA Modules:
  0.0 51.1 jit_solution(8157796315097244290)
XLA Ops:
  0.6 0.0 copy-start
  0.6 1.2 %copy-done = bf16[1,128,16,256]{3,2,1,0:T(8,128)(2,1)S(1)} copy-done((bf16[1,128,16,256]{3,2,1,0:T(8,128)(2,1)S(1)}, bf16[1,128,16,256]{3,2,1,0:T(8,128)(2,1)}, u32[]{:S(2)}) %copy-start) | copy-done | bytes 1048600
  1.9 0.0 copy-start.1
  1.9 1.1 %copy-done.1 = bf16[3,3,256,128]{3,2,1,0:T(8,128)(2,1)S(1)} copy-done((bf16[3,3,256,128]{3,2,1,0:T(8,128)(2,1)S(1)}, bf16[3,3,256,128]{3,2,1,0:T(8,128)(2,1)}, u32[]{:S(2)}) %copy-start.1) | copy-done | bytes 589848
  2.9 0.0 copy-start.2
  2.9 1.0 %copy-done.2 = bf16[1,64,32,128]{3,2,1,0:T(8,128)(2,1)S(1)} copy-done((bf16[1,64,32,128]{3,2,1,0:T(8,128)(2,1)S(1)}, bf16[1,64,32,128]{3,2,1,0:T(8,128)(2,1)}, u32[]{:S(2)}) %copy-start.2) | copy-done | bytes 524312
  4.0 45.3 %shard_map.50 = (bf16[64,32,128]{2,1,0:T(8,128)(2,1)S(1)}, f32[9,256,128]{2,1,0:T(8,128)S(1)}) custom-call(bf16[64,32,128]{2,1,0:T(8,128)(2,1)S(1)} %bitcast.9, bf16[128,16,256]{2,1,0:T(8,128)(2,1)S(1)} %bitcast.6, bf16[9,256,128]{2,1,0:T(8,128)(2,1)S(1)} %bitcast.7), custom_call_target="tpu_custom_call" | custom-call | tf_op jit(solution)/shard_map/pallas_call | solution.py:296
  49.3 0.8 %copy.7 = bf16[1,64,32,128]{3,2,1,0:T(8,128)(2,1)} copy(bf16[1,64,32,128]{3,2,1,0:T(8,128)(2,1)S(1)} %bitcast.8) | data formatting | bytes 1048576
  50.1 1.0 %copy.8 = f32[3,3,256,128]{3,2,1,0:T(8,128)} copy(f32[3,3,256,128]{3,2,1,0:T(8,128)S(1)} %bitcast.5) | data formatting | bytes 2359296
Async XLA Ops:
  0.6 1.2 %copy-start = (bf16[1,128,16,256]{3,2,1,0:T(8,128)(2,1)S(1)}, bf16[1,128,16,256]{3,2,1,0:T(8,128)(2,1)}, u32[]{:S(2)}) copy-start(bf16[1,128,16,256]{3,2,1,0:T(8,128)(2,1)} %param.4) | copy-start | bytes 3145732
  1.9 1.1 %copy-start.1 = (bf16[3,3,256,128]{3,2,1,0:T(8,128)(2,1)S(1)}, bf16[3,3,256,128]{3,2,1,0:T(8,128)(2,1)}, u32[]{:S(2)}) copy-start(bf16[3,3,256,128]{3,2,1,0:T(8,128)(2,1)} %param.5) | copy-start | bytes 1769476
  2.9 1.0 %copy-start.2 = (bf16[1,64,32,128]{3,2,1,0:T(8,128)(2,1)S(1)}, bf16[1,64,32,128]{3,2,1,0:T(8,128)(2,1)}, u32[]{:S(2)}) copy-start(bf16[1,64,32,128]{3,2,1,0:T(8,128)(2,1)} %param.3) | copy-start | bytes 1572868
